TPU v7x, 256 devices: a whole 4x4x8 slice. The times are simulated.
256 devices in a mesh: seq: 16 (over x, y), mp: 16 (over z, core).
Axes of the slice: x: 4, y: 4, z: 8, core: 2. Of those that a mesh axis runs over, the one named last changes fastest.
Arguments:
- hidden: bfloat16 [12288, 4096], P('seq', 'mp'), may hold values from -40 to 40
- encodings: bfloat16 [512, 256, 896], P('seq', 'mp'), may hold values from -32 to 32
- span_owner: int32 [192, 1], replicated, may hold values from 0 to 15; in each aligned block of 12 rows (0 to 11, 12 to 23, ...) at most 2 rows name the same one
- w_query: bfloat16 [4096, 4096], P(None, 'mp'), may hold values from -2 to 2
- w_key: bfloat16 [896, 4096], P(None, 'mp'), may hold values from -2 to 2
- w_value: bfloat16 [896, 4096], P(None, 'mp'), may hold values from -0.1875 to 0.1875
- w_out: bfloat16 [4096, 4096], P('mp'), may hold values from -0.5 to 0.5
- cotangent: bfloat16 [12288, 4096], P('seq', 'mp'), may hold values from -6 to 6
Outputs:
- branch: bfloat16 [12288, 4096], P('seq', 'mp')
- grad_hidden: bfloat16 [12288, 4096], P('seq', 'mp')
- grad_encodings: bfloat16 [512, 256, 896], P('seq', 'mp')
Inputs may be any that keep to these rules, and one draw needn't show every extreme that they name: `span_owner`: in each decoder shard's 12 spans (aligned blocks of rows) no encoder shard is named more than 2 times, and in every draw some shard of some block is named exactly 2 times.
All inputs are finite; a program needn't handle non-finite values.
Results may differ from a plain program's by a relative error of at most 0.025.
Values may be sent and summed in bfloat16 or wider, within the bound.
No kernel may reach another device: no remote copies, remote signals or barrier semaphores. Data moves between devices by JAX's collectives and lax.ppermute only.
A program may use at most 128 MiB of HBM per device.

v0:
```python
import jax
import jax.numpy as jnp
from jax import lax
from jax.sharding import PartitionSpec as P

DH = 128
SPAN = 64


def from_behind(value, axis, steps):
    count = lax.axis_size(axis)
    initial, last = (max(0, -steps), min(count, count - steps))
    return lax.ppermute(value, axis, [(source, source + steps) for source in range(initial, last)])


def attend(query_sets, key_sets, value_sets):
    scores = jnp.einsum(
        "sqhe,srhe->shqr", query_sets, key_sets, preferred_element_type=jnp.float32
    ) * DH ** (-0.5)
    highest = jnp.max(scores, axis=-1, keepdims=True)
    raised = jnp.exp(scores - highest)
    weights = raised / jnp.sum(raised, axis=-1, keepdims=True)
    weights_low = weights.astype(jnp.bfloat16)
    attended = jnp.einsum(
        "shqr,srhe->sqhe", weights_low, value_sets, preferred_element_type=jnp.float32
    ).astype(jnp.bfloat16)
    return (weights, weights_low, attended)


def attend_back(query_sets, key_sets, value_sets, weights, weights_low, grad_sets):
    grad_weights = jnp.einsum(
        "sqhe,srhe->shqr", grad_sets, value_sets, preferred_element_type=jnp.float32
    )
    inner_sum = jnp.sum(weights * grad_weights, axis=-1, keepdims=True)
    grad_scores = (weights * (grad_weights - inner_sum) * DH ** (-0.5)).astype(jnp.bfloat16)
    grad_queries = jnp.einsum(
        "shqr,srhe->sqhe", grad_scores, key_sets, preferred_element_type=jnp.float32
    )
    grad_keys = jnp.einsum(
        "shqr,sqhe->srhe", grad_scores, query_sets, preferred_element_type=jnp.float32
    )
    grad_values = jnp.einsum(
        "shqr,sqhe->srhe", weights_low, grad_sets, preferred_element_type=jnp.float32
    )
    return (grad_queries, grad_keys, grad_values)


def split_pairs(span_sets, columns):
    set_count = span_sets.shape[0]
    row_count = span_sets.shape[1]
    key_sets = span_sets[:, :, :columns].reshape(set_count, row_count, columns // DH, DH)
    value_sets = span_sets[:, :, columns:].reshape(set_count, row_count, columns // DH, DH)
    return (key_sets, value_sets)


def join_grads(grad_k_sets, grad_v_sets, columns):
    set_count = grad_k_sets.shape[0]
    row_count = grad_k_sets.shape[1]
    return jnp.concatenate(
        [
            grad_k_sets.reshape(set_count, row_count, columns),
            grad_v_sets.reshape(set_count, row_count, columns),
        ],
        axis=2,
    )


def on_device(hidden, encodings, span_owner, w_query, w_key, w_value, w_out, cotangent):
    seq_count = lax.axis_size("seq")
    shard_index = lax.axis_index("seq")
    capacity = encodings.shape[0] // seq_count
    token_count = hidden.shape[0]
    span_count = token_count // SPAN
    columns = w_query.shape[1]
    groups = columns // DH
    leading = SPAN - 1
    owners = lax.dynamic_slice_in_dim(span_owner[:, 0], shard_index * span_count, span_count)
    positions = jnp.arange(span_count, dtype=jnp.int32)
    earlier = (owners[:, None] == owners[None, :]) & (positions[None, :] < positions[:, None])
    picked = owners * capacity + jnp.sum(earlier.astype(jnp.int32), axis=1)
    both_weights = jnp.concatenate([w_key, w_value], axis=1)
    queries = jnp.dot(
        lax.all_gather(hidden, "mp", axis=1, tiled=True),
        w_query,
        preferred_element_type=jnp.float32,
    ).astype(jnp.bfloat16)
    grad_attended = lax.dot_general(
        lax.all_gather(cotangent, "mp", axis=1, tiled=True),
        w_out,
        (((1,), (1,)), ((), ())),
        preferred_element_type=jnp.float32,
    ).astype(jnp.bfloat16)
    received = lax.all_to_all(encodings, "seq", split_axis=0, concat_axis=0, tiled=True)
    every_row = lax.all_gather(received, "mp", axis=1, tiled=True)
    shard_part = jnp.take(every_row, picked, axis=0)
    flattened = shard_part.reshape(-1, shard_part.shape[2])
    projected = jnp.dot(flattened, both_weights, preferred_element_type=jnp.float32).astype(
        jnp.bfloat16
    )
    key_values = projected.reshape(shard_part.shape[0], shard_part.shape[1], 2 * columns)
    previous = from_behind(key_values[span_count - 1], "seq", 1)
    key_sets, value_sets = split_pairs(
        jnp.concatenate([previous[None], key_values], axis=0), columns
    )
    pad_front = jnp.zeros((1, columns), jnp.bfloat16)
    pad_back = jnp.zeros((leading, columns), jnp.bfloat16)
    query_sets = jnp.concatenate([pad_front, queries, pad_back], axis=0).reshape(
        span_count + 1, SPAN, groups, DH
    )
    grad_sets = jnp.concatenate([pad_front, grad_attended, pad_back], axis=0).reshape(
        span_count + 1, SPAN, groups, DH
    )
    weights, weights_low, attended_sets = attend(query_sets, key_sets, value_sets)
    attended = attended_sets.reshape(-1, columns)[1 : token_count + 1]
    grad_q_sets, grad_k_sets, grad_v_sets = attend_back(
        query_sets, key_sets, value_sets, weights, weights_low, grad_sets
    )
    grad_queries = grad_q_sets.reshape(-1, columns)[1 : token_count + 1].astype(jnp.bfloat16)
    grad_pairs = join_grads(grad_k_sets, grad_v_sets, columns)
    returned = from_behind(grad_pairs[0].astype(jnp.bfloat16), "seq", -1).astype(jnp.float32)
    grad_key_values = grad_pairs[1:].at[span_count - 1].add(returned)
    branch_terms = jnp.dot(attended, w_out, preferred_element_type=jnp.float32)
    branch = lax.psum_scatter(
        branch_terms.astype(jnp.bfloat16), "mp", scatter_dimension=1, tiled=True
    )
    hidden_terms = lax.dot_general(
        grad_queries, w_query, (((1,), (1,)), ((), ())), preferred_element_type=jnp.float32
    )
    grad_hidden = lax.psum_scatter(
        hidden_terms.astype(jnp.bfloat16), "mp", scatter_dimension=1, tiled=True
    )
    grad_low = grad_key_values.astype(jnp.bfloat16)
    shares = lax.psum_scatter(
        jnp.einsum(
            "crk,dk->rcd", grad_low, both_weights, preferred_element_type=jnp.float32
        ).astype(jnp.bfloat16),
        "mp",
        scatter_dimension=0,
        tiled=True,
    )
    outgoing = (
        jnp.zeros(encodings.shape, jnp.bfloat16).at[picked].set(jnp.transpose(shares, (1, 0, 2)))
    )
    grad_encodings = lax.all_to_all(outgoing, "seq", split_axis=0, concat_axis=0, tiled=True)
    return (branch, grad_hidden, grad_encodings)


def solution(mesh):
    return jax.shard_map(
        on_device,
        mesh=mesh,
        in_specs=(
            P("seq", "mp"),
            P("seq", "mp", None),
            P(),
            P(None, "mp"),
            P(None, "mp"),
            P(None, "mp"),
            P("mp", None),
            P("seq", "mp"),
        ),
        out_specs=(P("seq", "mp"), P("seq", "mp"), P("seq", "mp", None)),
        check_vma=False,
    )
```

profile of v0, /device:TPU:2, one launch (start us, length us, event | category | flops | bytes accessed | tf_op | source)
XLA Modules:
  0.0 503.8 jit_solution(15946810754894400640)
XLA Ops:
  7.2 0.0 all-gather.8.cloned.1.call-start
  7.2 0.7 all-gather.8.cloned.1.call-update
  7.9 0.0 all-gather.4.cloned.1.call-start
  8.0 21.3 %all_to_all.10 = bf16[32,16,896]{2,1,0:T(8,128)(2,1)} all-to-all(bf16[32,16,896]{2,1,0:T(8,128)(2,1)} %param.11), channel_id=1, replica_groups=mesh['seq'=16,'mp'=16] {'seq'}, dimensions={0} | all-to-all | bytes 1835008 | tf_op jit(solution)/shard_map/all_to_all | solution.py:93
  29.3 0.0 all-gather.6.cloned.1.call-start
  29.4 0.7 all-gather.6.cloned.1.call-update
  30.1 0.0 reduce-scatter.8.cloned.1.call-start
  30.1 0.1 fusion.46
  30.2 0.2 convert_reduce_fusion
  30.4 0.1 and_bitcast_fusion
  30.5 0.1 broadcast_in_dim.34
  30.6 0.1 pad.9.clone
  30.7 0.8 constant_dynamic-update-slice_fusion.1
  31.5 0.8 constant_dynamic-update-slice_fusion
  32.3 36.9 %all-gather.8.cloned.1.call-done = bf16[768,4096]{1,0:T(8,128)(2,1)} async-done(((bf16[768,256]{1,0:T(8,128)(2,1)}), bf16[768,4096]{1,0:T(8,128)(2,1)}) %all-gather.8.cloned.1.call-update) | async-done | bytes 6291472 | tf_op jit(solution)/shard_map/all_gather | solution.py:88
  69.2 4.6 convolution_convert_fusion.4
  73.8 81.0 %all-gather.4.cloned.1.call-done = bf16[32,256,896]{2,1,0:T(8,128)(2,1)} async-done(((bf16[32,16,896]{2,1,0:T(8,128)(2,1)}), bf16[32,256,896]{2,1,0:T(8,128)(2,1)}) %all-gather.4.cloned.1.call-update) | async-done | bytes 14680080 | tf_op jit(solution)/shard_map/all_gather | solution.py:94
  154.8 9.1 %gather_fusion = bf16[12,256,896]{2,1,0:T(8,128)(2,1)} fusion(bf16[32,256,896]{2,1,0:T(8,128)(2,1)} %all-gather.4.cloned.1.call-done, s32[1024]{0:T(1024)S(1)} %pad_clamp_fusion), kind=kCustom, calls=%fused_computation | custom fusion | bytes 11010096 | tf_op jit(solution)/shard_map/jit(_take)/gather | solution.py:95
  163.9 3.8 bitcast_select_fusion
  167.7 4.8 convolution_convert_fusion.2
  172.6 1.6 copy-done.6
  174.2 0.7 slice.57
  174.9 3.6 collective-permute-start
  178.5 33.0 %all-gather.6.cloned.1.call-done = bf16[768,4096]{1,0:T(8,128)(2,1)} async-done(((bf16[768,256]{1,0:T(8,128)(2,1)}), bf16[768,4096]{1,0:T(8,128)(2,1)}) %all-gather.6.cloned.1.call-update) | async-done | bytes 6291472 | tf_op jit(solution)/shard_map/all_gather | solution.py:83
  211.5 5.2 %convolution_convert_fusion.5 = bf16[768,256]{1,0:T(8,128)(2,1)S(1)} fusion(bf16[768,4096]{1,0:T(8,128)(2,1)} %all-gather.6.cloned.1.call-done, bf16[4096,256]{1,0:T(8,128)(2,1)} %param.13), kind=kOutput, calls=%fused_computation.32 | convolution fusion | flops 1610809344 | bytes 8781824 | tf_op jit(solution)/shard_map/dot_general | solution.py:82
  216.7 0.4 maximum_maximum_fusion.1
  217.1 0.1 reshape.88
  217.2 0.1 reshape.91
  217.3 4.7 copy.50
  222.0 1.1 copy.49
  223.1 2.2 pad_maximum_fusion
  225.3 0.4 fusion.40
  225.7 0.8 copy-done.4
  226.5 1.8 exponential_reduce_fusion
  228.3 1.6 fusion.37
  229.9 6.4 %fusion.31 = f32[13,2,128,256]{3,2,1,0:T(8,128)} fusion(bf16[13,64,2,128]{3,2,1,0:T(2,128)(2,1)S(1)} %reshape.91, f32[13,2,64]{2,1,0:T(2,128)S(1)} %get-tuple-element.21, f32[13,2,64,256]{3,2,1,0:T(8,128)} %copy-done.3), kind=kOutput, calls=%fused_computation.48 | convolution fusion | flops 110757760 | bytes 5544448 | tf_op jit(solution)/shard_map/shqr,sqhe->srhe/dot_general | solution.py:42
  236.3 14.3 %fusion.11 = f32[13,2,128,256]{3,2,1,0:T(8,128)} fusion(f32[13,2,64,256]{3,2,1,0:T(8,128)} %fusion.37, bf16[13,64,2,128]{3,2,1,0:T(2,128)(2,1)S(1)} %reshape.88, f32[13,2,64,256]{3,2,1,0:T(8,128)} %get-tuple-element.22, f32[13,2,64]{2,1,0:T(2,128)S(1)} %get-tuple-element.21), kind=kOutput, calls=%fused_computation.27 | convolution fusion | flops 112035712 | bytes 7248384 | tf_op jit(solution)/shard_map/shqr,sqhe->srhe/dot_general | solution.py:39
  250.6 4.7 copy.61
  255.3 4.7 copy.62
  260.1 1.2 fusion.42
  261.3 5.1 %collective-permute-start.1 = (bf16[256,512]{1,0:T(8,128)(2,1)S(1)}, bf16[256,512]{1,0:T(8,128)(2,1)S(1)}, u32[]{:S(2)}, u32[]{:S(2)}) collective-permute-start(bf16[256,512]{1,0:T(8,128)(2,1)S(1)} %fusion.42), channel_id=1, source_target_pairs={{16,0},{32,16},{48,32},{64,48},{80,64},{96,80},{112,96},{128,112},... | collective-permute-start | bytes 786440 | tf_op jit(solution)/shard_map/ppermute | solution.py:13
  266.4 0.4 fusion.2
  266.9 5.3 %collective-permute-done.1 = bf16[256,512]{1,0:T(8,128)(2,1)S(1)} collective-permute-done((bf16[256,512]{1,0:T(8,128)(2,1)S(1)}, bf16[256,512]{1,0:T(8,128)(2,1)S(1)}, u32[]{:S(2)}, u32[]{:S(2)}) %collective-permute-start.1) | collective-permute-done | bytes 262176 | tf_op jit(solution)/shard_map/ppermute | solution.py:13
  272.2 0.1 fusion.29
  272.2 6.0 %convert_bitcast_fusion = bf16[256,12,896]{0,2,1:T(8,128)(2,1)} fusion(bf16[12,256,512]{2,1,0:T(8,128)(2,1)S(1)} %fusion.29, bf16[896,512]{1,0:T(8,128)(2,1)} %constant_dynamic-update-slice_fusion), kind=kOutput, calls=%fused_computation.12 | convolution fusion | flops 2821324800 | bytes 9568256 | tf_op jit(solution)/shard_map/crk,dk->rcd/dot_general | solution.py:134
  278.2 11.4 %copy.63 = bf16[256,12,896]{2,1,0:T(8,128)(2,1)} copy(bf16[256,12,896]{0,2,1:T(8,128)(2,1)} %convert_bitcast_fusion) | data formatting | bytes 11010048 | tf_op jit(solution)/shard_map/convert_element_type | solution.py:136
  289.6 0.0 reduce-scatter.4.cloned.1.call-start
  289.7 4.9 fusion.22
  294.6 0.5 copy.54
  295.1 0.1 copy.82
  295.2 4.5 convolution_convert_fusion.1
  299.7 0.0 reduce-scatter.6.cloned.1.call-start
  299.7 12.9 %fusion.19 = bf16[13,64,2,128]{3,1,2,0:T(8,128)(2,1)S(1)} fusion(bf16[13,256,2,128]{1,3,2,0:T(8,128)(2,1)} %bitcast.62, f32[13,2,64,256]{3,2,1,0:T(8,128)} %fusion.37, f32[13,2,64,256]{3,2,1,0:T(8,128)} %get-tuple-element.22, f32[13,2,64]{2,1,0:T(2,128)S(1)} %get-tuple-element.21), kind=kOutput, calls=%fused_computation.33 | convolution fusion | flops 112248704 | bytes 5544448 | tf_op jit(solution)/shard_map/shqr,srhe->sqhe/dot_general | solution.py:36
  312.6 0.5 copy.58
  313.1 0.1 copy.81
  313.1 6.1 %convolution_convert_fusion = bf16[768,4096]{1,0:T(8,128)(2,1)} fusion(bf16[4096,256]{1,0:T(8,128)(2,1)} %param.13, bf16[832,256]{1,0:T(8,128)(2,1)S(1)} %bitcast.69), kind=kOutput, calls=%fused_computation.8 | convolution fusion | flops 1613758464 | bytes 8781824 | tf_op jit(solution)/shard_map/dot_general | solution.py:126
  319.2 39.1 %reduce-scatter.8.cloned.1.call-done = bf16[16,12,896]{2,1,0:T(8,128)(2,1)} async-done(((bf16[256,12,896]{2,1,0:T(8,128)(2,1)}), bf16[16,12,896]{2,1,0:T(8,128)(2,1)}) %reduce-scatter.8.cloned.1.call-update) | async-done | bytes 344080 | tf_op jit(solution)/shard_map/reduce_scatter | solution.py:133
  358.3 1.1 copy.64
  359.4 0.1 broadcast_in_dim.41
  359.5 1.0 scatter_fusion
  360.5 17.9 %all_to_all.11 = bf16[32,16,896]{2,1,0:T(8,128)(2,1)} all-to-all(bf16[32,16,896]{2,1,0:T(8,128)(2,1)S(1)} %scatter_fusion), channel_id=1, replica_groups=mesh['seq'=16,'mp'=16] {'seq'}, dimensions={0} | all-to-all | bytes 1835008 | tf_op jit(solution)/shard_map/all_to_all | solution.py:144
  378.4 48.6 %reduce-scatter.4.cloned.1.call-done = bf16[768,256]{1,0:T(8,128)(2,1)} async-done(((bf16[768,4096]{1,0:T(8,128)(2,1)}), bf16[768,256]{1,0:T(8,128)(2,1)}) %reduce-scatter.4.cloned.1.call-update) | async-done | bytes 393232 | tf_op jit(solution)/shard_map/reduce_scatter | solution.py:123
  426.9 67.9 %reduce-scatter.6.cloned.1.call-done = bf16[768,256]{1,0:T(8,128)(2,1)} async-done(((bf16[768,4096]{1,0:T(8,128)(2,1)}), bf16[768,256]{1,0:T(8,128)(2,1)}) %reduce-scatter.6.cloned.1.call-update) | async-done | bytes 393232 | tf_op jit(solution)/shard_map/reduce_scatter | solution.py:129
  494.8 2.2 copy.87
  (27 shorter events, 0.1 us)
Async XLA Ops:
  7.2 62.0 %copy-start = (bf16[256,4096]{1,0:T(8,128)(2,1)S(1)}, bf16[256,4096]{1,0:T(8,128)(2,1)}, u32[]{:S(2)}) copy-start(bf16[256,4096]{1,0:T(8,128)(2,1)} %param.16) | copy-start | bytes 6291460
  7.2 22.9 %copy-start.9 = (s32[192,1]{0,1:T(1,128)S(1)}, s32[192,1]{0,1:T(1,128)}, u32[]{:S(2)}) copy-start(s32[192,1]{0,1:T(1,128)} %param.12) | copy-start | bytes 2308
  7.2 23.5 %copy-start.7 = (bf16[896,256]{1,0:T(8,128)(2,1)S(1)}, bf16[896,256]{1,0:T(8,128)(2,1)}, u32[]{:S(2)}) copy-start(bf16[896,256]{1,0:T(8,128)(2,1)} %param.14) | copy-start | bytes 1376260
  7.2 62.0 %all-gather.8.cloned.1.call-start = ((), (), s32[]{:S(2)}) async-start(), calls=%async_computation.8 | async-start | bytes 6684672 | tf_op jit(solution)/shard_map/all_gather | solution.py:88
  7.9 23.6 %copy-start.8 = (bf16[896,256]{1,0:T(8,128)(2,1)S(1)}, bf16[896,256]{1,0:T(8,128)(2,1)}, u32[]{:S(2)}) copy-start(bf16[896,256]{1,0:T(8,128)(2,1)} %param.15) | copy-start | bytes 1376260
  7.9 146.8 %all-gather.4.cloned.1.call-start = ((), (), s32[]{:S(2)}) async-start(), calls=%async_computation.5 | async-start | bytes 15597568 | tf_op jit(solution)/shard_map/all_gather | solution.py:94
  29.3 182.2 %all-gather.6.cloned.1.call-start = ((), (), s32[]{:S(2)}) async-start(), calls=%async_computation.6 | async-start | bytes 6684672 | tf_op jit(solution)/shard_map/all_gather | solution.py:83
  30.1 328.2 %reduce-scatter.8.cloned.1.call-start = ((), (), s32[]{:S(2)}) async-start(), calls=%async_computation.10 | async-start | bytes 7798784 | tf_op jit(solution)/shard_map/reduce_scatter | solution.py:133
  172.6 1.7 copy-start.6
  174.9 47.1 %collective-permute-start = (bf16[256,512]{1,0:T(8,128)(2,1)}, bf16[256,512]{1,0:T(8,128)(2,1)}, u32[]{:S(2)}, u32[]{:S(2)}) collective-permute-start(bf16[256,512]{1,0:T(8,128)(2,1)} %slice.57), channel_id=1, source_target_pairs={{0,16},{16,32},{32,48},{48,64},{64,80},{80,96},{96,112},{112,128},... | collective-permute-start | bytes 786440 | tf_op jit(solution)/shard_map/ppermute | solution.py:13
  225.3 1.2 copy-start.4
  225.3 2.9 copy-start.5
  226.5 1.8 copy-start.3
  260.1 6.4 %copy-start.1 = (f32[13,256,256]{2,1,0:T(8,128)S(1)}, f32[13,256,256]{2,1,0:T(8,128)}, u32[]{:S(2)}) copy-start(f32[13,256,256]{2,1,0:T(8,128)} %copy.61) | copy-start | bytes 10223620
  260.1 6.4 %copy-start.2 = (f32[13,256,256]{2,1,0:T(8,128)S(1)}, f32[13,256,256]{2,1,0:T(8,128)}, u32[]{:S(2)}) copy-start(f32[13,256,256]{2,1,0:T(8,128)} %copy.62) | copy-start | bytes 10223620
  261.3 10.9 %collective-permute-start.1 = (bf16[256,512]{1,0:T(8,128)(2,1)S(1)}, bf16[256,512]{1,0:T(8,128)(2,1)S(1)}, u32[]{:S(2)}, u32[]{:S(2)}) collective-permute-start(bf16[256,512]{1,0:T(8,128)(2,1)S(1)} %fusion.42), channel_id=1, source_target_pairs={{16,0},{32,16},{48,32},{64,48},{80,64},{96,80},{112,96},{128,112},... | collective-permute-start | bytes 786440 | tf_op jit(solution)/shard_map/ppermute | solution.py:13
  289.6 137.3 %reduce-scatter.4.cloned.1.call-start = ((), (), s32[]{:S(2)}) async-start(), calls=%async_computation.7 | async-start | bytes 6684672 | tf_op jit(solution)/shard_map/reduce_scatter | solution.py:123
  299.7 195.1 %reduce-scatter.6.cloned.1.call-start = ((), (), s32[]{:S(2)}) async-start(), calls=%async_computation.9 | async-start | bytes 6684672 | tf_op jit(solution)/shard_map/reduce_scatter | solution.py:129
Sparse Core Ops, SparseCore 0:
  9.8 59.3 all-gather.7
  71.0 83.7 all-gather.3
  156.6 54.9 all-gather.5
  289.8 68.5 reduce-scatter.7
  361.3 65.5 reduce-scatter.3
  429.9 64.8 reduce-scatter.5
where the time goes:
time: 505 us; the launch traced here: 504 us
  waiting for transfers between devices  313 us (62%)
  matrix products  71.7 us (14%)
  local copies, waits for them, and re-layouts  46.3 us (9%)
  blocking collectives  39.2 us (8%)
  between operations  14.4 us (3%)
  other arithmetic  10.1 us (2%)
  starting transfers between devices  8.93 us (2%)
    all_gather x1, waiting for transfers between devices, on_device(): every_row = lax.all_gather(received, 'mp', axis=1, tiled=True)  81 us
    reduce_scatter x1, waiting for transfers between devices, on_device(): lax.psum_scatter(hidden_terms.astype(jnp.bfloat16), 'mp', scatter_dimensi...  67.9 us
    reduce_scatter x1, waiting for transfers between devices, on_device(): lax.psum_scatter(branch_terms.astype(jnp.bfloat16), 'mp', scatter_dimensi...  48.6 us
    reduce_scatter x1, waiting for transfers between devices, on_device(): lax.psum_scatter(jnp.einsum('crk,dk->rcd', grad_low, both_weights, prefer...  39.1 us
    all_gather x1, waiting for transfers between devices, on_device(): lax.all_gather(cotangent, 'mp', axis=1, tiled=True)  36.9 us
    all_gather x1, waiting for transfers between devices, on_device(): lax.all_gather(hidden, 'mp', axis=1, tiled=True)  33 us
    all_to_all x1, blocking collectives, on_device(): lax.all_to_all(encodings, 'seq', split_axis=0, concat_axis=0, tiled=True)  21.3 us
    all_to_all x1, blocking collectives, on_device(): lax.all_to_all(outgoing, 'seq', split_axis=0, concat_axis=0, tiled=True)  17.9 us
  transfers between devices with their start and end apart: 8, of which 7 were waited for; matrix products, arithmetic and copies ran while one was open for 13% of the time, Pallas kernels for 0%

commit v1 on v0

--- a/solution.py
+++ b/solution.py
@@ -85,7 +85,9 @@
         preferred_element_type=jnp.float32,
     ).astype(jnp.bfloat16)
     grad_attended = lax.dot_general(
-        lax.all_gather(cotangent, "mp", axis=1, tiled=True),
+        jnp.concatenate(
+            lax.all_to_all(jnp.stack([cotangent] * lax.axis_size("mp")), "mp", 0, 0), axis=1
+        ),
         w_out,
         (((1,), (1,)), ((), ())),
         preferred_element_type=jnp.float32,

time: 505 us -> 599 us (1.19)
  waiting for transfers between devices: 313 us -> 396 us
  starting transfers between devices: 8.93 us -> 16.8 us
    all_to_all x0 -> x1, waiting for transfers between devices: none -> 197 us  [on_device(): lax.all_to_all(jnp.stack([cotangent] * lax.axis_size('mp')), 'mp', 0, 0)]
    all_gather x1, waiting for transfers between devices: 81 us -> 4.95 us  [on_device(): every_row = lax.all_gather(received, 'mp', axis=1, tiled=True)]
    all_gather x1 -> x0, waiting for transfers between devices: 36.9 us -> none  [on_device(): lax.all_gather(cotangent, 'mp', axis=1, tiled=True)]
    all_to_all x0 -> x1, starting transfers between devices: none -> 8.75 us  [on_device(): lax.all_to_all(jnp.stack([cotangent] * lax.axis_size('mp')), 'mp', 0, 0)]
  transfers between devices with their start and end apart: 8 -> 8, of which waited for: 7 -> 7; matrix products, arithmetic and copies ran while one was open for 13% -> 12% of each run, Pallas kernels for 0% -> 0%
where the time goes in v1:
time: 599 us; the launch traced here: 598 us
  waiting for transfers between devices  396 us (66%)
  matrix products  71.8 us (12%)
  local copies, waits for them, and re-layouts  49.7 us (8%)
  blocking collectives  39 us (7%)
  starting transfers between devices  16.8 us (3%)
  between operations  14.1 us (2%)
  other arithmetic  10 us (2%)
    all_to_all x1, waiting for transfers between devices, on_device(): lax.all_to_all(jnp.stack([cotangent] * lax.axis_size('mp')), 'mp', 0, 0)  197 us
    reduce_scatter x1, waiting for transfers between devices, on_device(): lax.psum_scatter(hidden_terms.astype(jnp.bfloat16), 'mp', scatter_dimensi...  67.9 us
    reduce_scatter x1, waiting for transfers between devices, on_device(): lax.psum_scatter(branch_terms.astype(jnp.bfloat16), 'mp', scatter_dimensi...  48.5 us
    reduce_scatter x1, waiting for transfers between devices, on_device(): lax.psum_scatter(jnp.einsum('crk,dk->rcd', grad_low, both_weights, prefer...  39.1 us
    all_gather x1, waiting for transfers between devices, on_device(): lax.all_gather(hidden, 'mp', axis=1, tiled=True)  32.9 us
    all_to_all x1, blocking collectives, on_device(): lax.all_to_all(encodings, 'seq', split_axis=0, concat_axis=0, tiled=True)  21.3 us
    all_to_all x1, blocking collectives, on_device(): lax.all_to_all(outgoing, 'seq', split_axis=0, concat_axis=0, tiled=True)  17.7 us
    dot_general x1, matrix products, attend_back(): jnp.einsum('shqr,sqhe->srhe', grad_scores, query_sets, preferred_element_...  14.3 us
  transfers between devices with their start and end apart: 8, of which 7 were waited for; matrix products, arithmetic and copies ran while one was open for 12% of the time, Pallas kernels for 0%

profile of v1, /device:TPU:2, one launch (start us, length us, event | category | flops | bytes accessed | tf_op | source)
XLA Modules:
  0.0 597.8 jit_solution(12023099582701534982)
XLA Ops:
  7.2 21.3 %all_to_all.15 = bf16[32,16,896]{2,1,0:T(8,128)(2,1)} all-to-all(bf16[32,16,896]{2,1,0:T(8,128)(2,1)} %param.11), channel_id=1, replica_groups=mesh['seq'=16,'mp'=16] {'seq'}, dimensions={0} | all-to-all | bytes 1835008 | tf_op jit(solution)/shard_map/all_to_all | solution.py:95
  28.6 0.2 copy.57
  28.8 3.2 stack.2
  32.0 8.7 %all-to-all-start.1 = ((bf16[16,768,256]{1,2,0:T(8,128)(2,1)}), bf16[16,768,256]{1,2,0:T(8,128)(2,1)}, u32[]{:S(2)}, u32[]{:S(2)}) async-start(bf16[16,768,256]{1,2,0:T(8,128)(2,1)} %stack.2), calls=%async_computation.2 | async-start | bytes 12582912 | tf_op jit(solution)/shard_map/all_to_all | solution.py:89
  40.7 0.0 all-gather.5.cloned.1.call-start
  40.8 0.7 all-gather.5.cloned.1.call-update
  41.5 0.0 reduce-scatter.8.cloned.1.call-start
  41.5 0.1 fusion.46
  41.6 0.2 convert_reduce_fusion
  41.8 0.1 and_bitcast_fusion
  41.9 0.1 broadcast_in_dim.34
  42.0 0.1 pad.9.clone
  42.1 0.8 constant_dynamic-update-slice_fusion.1
  42.9 0.8 constant_dynamic-update-slice_fusion
  43.7 196.8 %all-to-all-done.1 = bf16[16,768,256]{1,2,0:T(8,128)(2,1)} async-done(((bf16[16,768,256]{1,2,0:T(8,128)(2,1)}), bf16[16,768,256]{1,2,0:T(8,128)(2,1)}, u32[]{:S(2)}, u32[]{:S(2)}) %all-to-all-start.1) | async-done | bytes 6291488 | tf_op jit(solution)/shard_map/all_to_all | solution.py:89
  240.5 4.7 convolution_convert_fusion.4
  245.2 5.0 all-gather.3.cloned.1.call-done
  250.2 9.1 %gather_fusion = bf16[12,256,896]{2,1,0:T(8,128)(2,1)} fusion(bf16[32,256,896]{2,1,0:T(8,128)(2,1)} %all-gather.3.cloned.1.call-done, s32[1024]{0:T(1024)S(1)} %pad_clamp_fusion), kind=kCustom, calls=%fused_computation | custom fusion | bytes 11010096 | tf_op jit(solution)/shard_map/jit(_take)/gather | solution.py:97
  259.3 3.8 bitcast_select_fusion
  263.0 4.8 convolution_convert_fusion.2
  267.9 1.6 copy-done.6
  269.5 0.7 slice.57
  270.2 2.8 collective-permute-start
  273.0 32.9 %all-gather.5.cloned.1.call-done = bf16[768,4096]{1,0:T(8,128)(2,1)} async-done(((bf16[768,256]{1,0:T(8,128)(2,1)}), bf16[768,4096]{1,0:T(8,128)(2,1)}) %all-gather.5.cloned.1.call-update) | async-done | bytes 6291472 | tf_op jit(solution)/shard_map/all_gather | solution.py:83
  305.9 5.2 convolution_convert_fusion.5
  311.1 0.4 maximum_maximum_fusion.1
  311.5 0.1 reshape.96
  311.6 0.1 reshape.101
  311.7 4.7 copy.52
  316.4 1.1 copy.51
  317.5 2.2 pad_maximum_fusion
  319.7 0.4 fusion.40
  320.1 0.8 copy-done.4
  320.9 1.8 exponential_reduce_fusion
  322.6 1.6 fusion.37
  324.2 6.4 %fusion.31 = f32[13,2,128,256]{3,2,1,0:T(8,128)} fusion(bf16[13,64,2,128]{3,2,1,0:T(2,128)(2,1)S(1)} %reshape.101, f32[13,2,64]{2,1,0:T(2,128)S(1)} %get-tuple-element.21, f32[13,2,64,256]{3,2,1,0:T(8,128)} %copy-done.3), kind=kOutput, calls=%fused_computation.48 | convolution fusion | flops 110757760 | bytes 5544448 | tf_op jit(solution)/shard_map/shqr,sqhe->srhe/dot_general | solution.py:42
  330.7 14.3 %fusion.11 = f32[13,2,128,256]{3,2,1,0:T(8,128)} fusion(f32[13,2,64,256]{3,2,1,0:T(8,128)} %fusion.37, bf16[13,64,2,128]{3,2,1,0:T(2,128)(2,1)S(1)} %reshape.96, f32[13,2,64,256]{3,2,1,0:T(8,128)} %get-tuple-element.22, f32[13,2,64]{2,1,0:T(2,128)S(1)} %get-tuple-element.21), kind=kOutput, calls=%fused_computation.27 | convolution fusion | flops 112035712 | bytes 7248384 | tf_op jit(solution)/shard_map/shqr,sqhe->srhe/dot_general | solution.py:39
  345.0 4.7 copy.64
  349.7 4.7 copy.65
  354.4 1.2 fusion.42
  355.6 5.1 collective-permute-start.1
  360.8 0.4 fusion.2
  361.2 5.3 collective-permute-done.1
  366.5 0.1 fusion.29
  366.6 6.0 %convert_bitcast_fusion = bf16[256,12,896]{0,2,1:T(8,128)(2,1)} fusion(bf16[12,256,512]{2,1,0:T(8,128)(2,1)S(1)} %fusion.29, bf16[896,512]{1,0:T(8,128)(2,1)} %constant_dynamic-update-slice_fusion), kind=kOutput, calls=%fused_computation.12 | convolution fusion | flops 2821324800 | bytes 9568256 | tf_op jit(solution)/shard_map/crk,dk->rcd/dot_general | solution.py:136
  372.6 11.4 %copy.66 = bf16[256,12,896]{2,1,0:T(8,128)(2,1)} copy(bf16[256,12,896]{0,2,1:T(8,128)(2,1)} %convert_bitcast_fusion) | data formatting | bytes 11010048 | tf_op jit(solution)/shard_map/convert_element_type | solution.py:138
  384.0 0.0 reduce-scatter.4.cloned.1.call-start
  384.1 4.9 fusion.22
  389.0 0.5 copy.56
  389.5 0.1 copy.85
  389.5 4.5 convolution_convert_fusion.1
  394.1 0.0 reduce-scatter.6.cloned.1.call-start
  394.1 12.9 %fusion.19 = bf16[13,64,2,128]{3,1,2,0:T(8,128)(2,1)S(1)} fusion(bf16[13,256,2,128]{1,3,2,0:T(8,128)(2,1)} %bitcast.65, f32[13,2,64,256]{3,2,1,0:T(8,128)} %fusion.37, f32[13,2,64,256]{3,2,1,0:T(8,128)} %get-tuple-element.22, f32[13,2,64]{2,1,0:T(2,128)S(1)} %get-tuple-element.21), kind=kOutput, calls=%fused_computation.33 | convolution fusion | flops 112248704 | bytes 5544448 | tf_op jit(solution)/shard_map/shqr,srhe->sqhe/dot_general | solution.py:36
  407.0 0.5 copy.61
  407.4 0.1 copy.84
  407.5 6.1 %convolution_convert_fusion = bf16[768,4096]{1,0:T(8,128)(2,1)} fusion(bf16[4096,256]{1,0:T(8,128)(2,1)} %param.13, bf16[832,256]{1,0:T(8,128)(2,1)S(1)} %bitcast.72), kind=kOutput, calls=%fused_computation.8 | convolution fusion | flops 1613758464 | bytes 8781824 | tf_op jit(solution)/shard_map/dot_general | solution.py:128
  413.6 39.1 %reduce-scatter.8.cloned.1.call-done = bf16[16,12,896]{2,1,0:T(8,128)(2,1)} async-done(((bf16[256,12,896]{2,1,0:T(8,128)(2,1)}), bf16[16,12,896]{2,1,0:T(8,128)(2,1)}) %reduce-scatter.8.cloned.1.call-update) | async-done | bytes 344080 | tf_op jit(solution)/shard_map/reduce_scatter | solution.py:135
  452.7 1.1 copy.67
  453.8 0.1 broadcast_in_dim.41
  453.9 1.0 scatter_fusion
  454.9 17.7 %all_to_all.16 = bf16[32,16,896]{2,1,0:T(8,128)(2,1)} all-to-all(bf16[32,16,896]{2,1,0:T(8,128)(2,1)S(1)} %scatter_fusion), channel_id=1, replica_groups=mesh['seq'=16,'mp'=16] {'seq'}, dimensions={0} | all-to-all | bytes 1835008 | tf_op jit(solution)/shard_map/all_to_all | solution.py:146
  472.6 48.5 %reduce-scatter.4.cloned.1.call-done = bf16[768,256]{1,0:T(8,128)(2,1)} async-done(((bf16[768,4096]{1,0:T(8,128)(2,1)}), bf16[768,256]{1,0:T(8,128)(2,1)}) %reduce-scatter.4.cloned.1.call-update) | async-done | bytes 393232 | tf_op jit(solution)/shard_map/reduce_scatter | solution.py:125
  521.1 67.9 %reduce-scatter.6.cloned.1.call-done = bf16[768,256]{1,0:T(8,128)(2,1)} async-done(((bf16[768,4096]{1,0:T(8,128)(2,1)}), bf16[768,256]{1,0:T(8,128)(2,1)}) %reduce-scatter.6.cloned.1.call-update) | async-done | bytes 393232 | tf_op jit(solution)/shard_map/reduce_scatter | solution.py:131
  589.1 2.2 copy.90
  (30 shorter events, 0.2 us)
Async XLA Ops:
  7.2 233.4 %copy-start = (bf16[256,4096]{1,0:T(8,128)(2,1)S(1)}, bf16[256,4096]{1,0:T(8,128)(2,1)}, u32[]{:S(2)}) copy-start(bf16[256,4096]{1,0:T(8,128)(2,1)} %param.16) | copy-start | bytes 6291460
  7.2 21.4 %copy-start.9 = (bf16[768,256]{1,0:T(8,128)(2,1)S(1)}, bf16[768,256]{1,0:T(8,128)(2,1)}, u32[]{:S(2)}) copy-start(bf16[768,256]{1,0:T(8,128)(2,1)} %param.17) | copy-start | bytes 1179652
  7.2 243.0 %all-gather.3.cloned.1.call-start = ((), (), s32[]{:S(2)}) async-start(), calls=%async_computation.6 | async-start | bytes 15597568 | tf_op jit(solution)/shard_map/all_gather | solution.py:96
  32.0 9.6 %copy-start.10 = (s32[192,1]{0,1:T(1,128)S(1)}, s32[192,1]{0,1:T(1,128)}, u32[]{:S(2)}) copy-start(s32[192,1]{0,1:T(1,128)} %param.12) | copy-start | bytes 2308
  32.0 10.1 %copy-start.7 = (bf16[896,256]{1,0:T(8,128)(2,1)S(1)}, bf16[896,256]{1,0:T(8,128)(2,1)}, u32[]{:S(2)}) copy-start(bf16[896,256]{1,0:T(8,128)(2,1)} %param.14) | copy-start | bytes 1376260
  32.0 10.9 %copy-start.8 = (bf16[896,256]{1,0:T(8,128)(2,1)S(1)}, bf16[896,256]{1,0:T(8,128)(2,1)}, u32[]{:S(2)}) copy-start(bf16[896,256]{1,0:T(8,128)(2,1)} %param.15) | copy-start | bytes 1376260
  32.0 208.5 %all-to-all-start.1 = ((bf16[16,768,256]{1,2,0:T(8,128)(2,1)}), bf16[16,768,256]{1,2,0:T(8,128)(2,1)}, u32[]{:S(2)}, u32[]{:S(2)}) async-start(bf16[16,768,256]{1,2,0:T(8,128)(2,1)} %stack.2), calls=%async_computation.2 | async-start | bytes 12582912 | tf_op jit(solution)/shard_map/all_to_all | solution.py:89
  40.7 265.2 %all-gather.5.cloned.1.call-start = ((), (), s32[]{:S(2)}) async-start(), calls=%async_computation.7 | async-start | bytes 6684672 | tf_op jit(solution)/shard_map/all_gather | solution.py:83
  41.5 411.3 %reduce-scatter.8.cloned.1.call-start = ((), (), s32[]{:S(2)}) async-start(), calls=%async_computation.10 | async-start | bytes 7798784 | tf_op jit(solution)/shard_map/reduce_scatter | solution.py:135
  267.9 1.7 copy-start.6
  270.2 46.1 %collective-permute-start = (bf16[256,512]{1,0:T(8,128)(2,1)}, bf16[256,512]{1,0:T(8,128)(2,1)}, u32[]{:S(2)}, u32[]{:S(2)}) collective-permute-start(bf16[256,512]{1,0:T(8,128)(2,1)} %slice.57), channel_id=1, source_target_pairs={{0,16},{16,32},{32,48},{48,64},{64,80},{80,96},{96,112},{112,128},... | collective-permute-start | bytes 786440 | tf_op jit(solution)/shard_map/ppermute | solution.py:13
  319.7 1.2 copy-start.4
  319.7 2.9 copy-start.5
  320.9 1.8 copy-start.3
  354.4 6.4 %copy-start.1 = (f32[13,256,256]{2,1,0:T(8,128)S(1)}, f32[13,256,256]{2,1,0:T(8,128)}, u32[]{:S(2)}) copy-start(f32[13,256,256]{2,1,0:T(8,128)} %copy.64) | copy-start | bytes 10223620
  354.4 6.4 %copy-start.2 = (f32[13,256,256]{2,1,0:T(8,128)S(1)}, f32[13,256,256]{2,1,0:T(8,128)}, u32[]{:S(2)}) copy-start(f32[13,256,256]{2,1,0:T(8,128)} %copy.65) | copy-start | bytes 10223620
  355.6 10.9 %collective-permute-start.1 = (bf16[256,512]{1,0:T(8,128)(2,1)S(1)}, bf16[256,512]{1,0:T(8,128)(2,1)S(1)}, u32[]{:S(2)}, u32[]{:S(2)}) collective-permute-start(bf16[256,512]{1,0:T(8,128)(2,1)S(1)} %fusion.42), channel_id=1, source_target_pairs={{16,0},{32,16},{48,32},{64,48},{80,64},{96,80},{112,96},{128,112},... | collective-permute-start | bytes 786440 | tf_op jit(solution)/shard_map/ppermute | solution.py:13
  384.0 137.1 %reduce-scatter.4.cloned.1.call-start = ((), (), s32[]{:S(2)}) async-start(), calls=%async_computation.8 | async-start | bytes 6684672 | tf_op jit(solution)/shard_map/reduce_scatter | solution.py:125
  394.1 195.0 %reduce-scatter.6.cloned.1.call-start = ((), (), s32[]{:S(2)}) async-start(), calls=%async_computation.9 | async-start | bytes 6684672 | tf_op jit(solution)/shard_map/reduce_scatter | solution.py:131
Sparse Core Ops, SparseCore 0:
  28.7 221.4 all-gather.2
  251.9 53.9 all-gather.4
  384.1 68.5 reduce-scatter.7
  455.7 65.3 reduce-scatter.3
  524.1 64.8 reduce-scatter.5
